TPU v7x, 32 devices: a whole 2x2x4 slice. The times are simulated.
32 devices in a mesh: row: 16 (over z, x, core), col: 2 (over y).
Axes of the slice: x: 2, y: 2, z: 4, core: 2. Of those that a mesh axis runs over, the one named last changes fastest.
Arguments:
- covariance: float32 [16384, 16384], P('row', 'col'), may hold values from -6 to 6
- lon_courant: float32 [128, 128], replicated, may hold values from 0.05 to 0.95
- lat_courant: float32 [128, 128], replicated, may hold values from 0.05 to 0.9
- zonal_upwind_sign: int32 [128, 128], replicated, may hold values 0 or 1
- lat_sign: int32 [128, 128], replicated, may hold values 0 or 1
- cycle_counts: int32 [128], replicated, may hold values from 1 to 4
Outputs:
- forecast: float32 [16384, 16384], P('row', 'col')
Inputs may be any that keep to these rules, and one draw needn't show every extreme that they name: `zonal_upwind_sign`: 1 where the wind blows toward growing longitude, 0 otherwise. `lat_sign`: 1 where the wind blows toward growing latitude, 0 otherwise.
All inputs are finite; a program needn't handle non-finite values.
Results may differ from a plain program's by a relative error of at most 0.00002.
Values sent between devices are 32-bit elements; how exact they have to be, the bound alone decides.
No kernel may reach another device: no remote copies, remote signals or barrier semaphores. Data moves between devices by JAX's collectives and lax.ppermute only.
A program may use at most 320 MiB of HBM per device.

v0:
```python
import functools

import jax
import jax.numpy as jnp
from jax import lax
from jax.experimental import pallas as pl
from jax.experimental.pallas import tpu as pltpu
from jax.sharding import PartitionSpec as P

SUBCYCLES = 4
F32, BF16 = jnp.float32, jnp.bfloat16
LON_RATE, LAT_RATE, ZONAL, HEADING, COUNTS = range(5)
VMEM_BYTES = 56 * 1024 * 1024
HIGHEST = lax.Precision.HIGHEST


def split(values):
    high = values.astype(BF16)
    return high, (values - high.astype(F32)).astype(BF16)


def dot(left, right):
    return jnp.dot(left, right, preferred_element_type=F32)


def exact_dot(left, right):
    return jnp.dot(left, right, preferred_element_type=F32, precision=HIGHEST)


def blend(center, rate, sign, below, above):
    return center - rate * (center - jnp.where(sign > 0.5, below, above))


def table_row(tables, which, at):
    return tables[which, pl.ds(at, 1), :]


def zonal_bands(rate, sign, count):
    lons = rate.shape[-1]
    zero = jnp.zeros_like(rate)
    bands = {0: jnp.ones_like(rate)}
    for cycle in range(SUBCYCLES):
        cell = jnp.where(count > cycle, rate, 0.0)
        west = {k - 1: pltpu.roll(band, 1, 1) for k, band in bands.items()}
        east = {k + 1: pltpu.roll(band, lons - 1, 1) for k, band in bands.items()}
        bands = {
            k: blend(bands.get(k, zero), cell, sign, west.get(k, zero), east.get(k, zero))
            for k in range(-cycle - 1, cycle + 2)
        }
    return bands


def zonal_matrix(bands, lat):
    lons = bands[0].shape[-1]
    reach = lax.broadcasted_iota(jnp.int32, (lons, lons), 0) - lax.broadcasted_iota(jnp.int32, (lons, lons), 1)
    reach = jnp.where(reach < 0, reach + lons, reach)
    field = jnp.zeros((lons, lons), F32)
    for k, band in bands.items():
        field = jnp.where(reach == k % lons, band[lat:lat + 1, :], field)
    return field


def column_tables_kernel(tables, out):
    lons = tables.shape[-1]
    bands = zonal_bands(tables[LON_RATE], tables[ZONAL], tables[COUNTS])
    for lat in range(out.shape[0]):
        high, low = split(zonal_matrix(bands, lat))
        out[lat, :lons, :lons] = high
        out[lat, :lons, lons:] = low
        out[lat, lons:, :lons] = high
        out[lat, lons:, lons:] = jnp.zeros_like(low)


def padded(count, least):
    return -(-count // least) * least


def prepare_kernel(firsts, *refs):
    sources, (row_part, col_part, first_part, mat_part, most, wide) = refs[:5], refs[5:]
    lats, lons = sources[0].shape
    wide[...] = jnp.zeros_like(wide)
    for which, source in enumerate(sources):
        wide[which, 8:8 + lats, :] = jnp.broadcast_to(source[...].astype(F32), (lats, lons))
    row_lats = row_part.shape[1] - 4
    for which in range(5):
        for out, first in ((row_part, firsts[0] + 6), (col_part, firsts[1] + 6), (first_part, firsts[2] + 7),
                           (mat_part, firsts[1] + 7)):
            out[which] = wide[which, pl.ds(first, out.shape[1]), :]
    heading = (sources[HEADING][...] == 1).astype(F32)
    upward = jnp.sum(heading, axis=1, keepdims=True)
    lat = lax.broadcasted_iota(jnp.int32, (lats, 1), 0)
    place = lat % (2 * row_lats)
    low = (place == 0) & (lat > 0)
    high = (place == 2 * row_lats - 1) & (lat < lats - 1)
    needed = jnp.where(low, upward, jnp.where(high, lons - upward, 0.0))
    most[0] = jnp.max(needed).astype(jnp.int32)


def row_tables_kernel(kept, blocks, tables, mats, rates, signs, pack_cross, pack_chip, add_cross, add_chip):
    lons = tables.shape[-1]
    lats = mats.shape[0] - 2
    square = (lons, lons)
    down = lax.broadcasted_iota(jnp.int32, square, 0)
    across = lax.broadcasted_iota(jnp.int32, square, 1)

    def spread(which, at):
        return jnp.broadcast_to(table_row(tables, which, at), square).T

    low_mat = high_mat = None
    bands = zonal_bands(tables[LON_RATE], tables[ZONAL], tables[COUNTS])
    for lat in range(lats + 2):
        mat = zonal_matrix(bands, lat + 1).T
        if lat == 1:
            low_mat = mat
        if lat == lats:
            high_mat = mat
        high, low = split(mat)
        mats[lat, :lons, :lons] = high
        mats[lat, :lons, lons:] = high
        mats[lat, lons:, :lons] = low
        mats[lat, lons:, lons:] = jnp.zeros_like(low)
        rates[lat] = spread(LAT_RATE, lat + 1)
        signs[lat] = spread(HEADING, lat + 1)

    def packer(out, size, is_low):
        edge, beyond = (2, 1) if is_low else (lats + 1, lats + 2)
        mat = low_mat if is_low else high_mat
        wanted = not is_low
        rows = padded(2 * size, 16)
        sign = jnp.broadcast_to(table_row(tables, HEADING, beyond), square)
        mask = (sign > 0.5) == wanted
        rank = dot(mask.astype(BF16), (down <= across).astype(BF16))
        rank = jnp.where(mask, rank, 0.0)[:1]
        spot = lax.broadcasted_iota(jnp.int32, (rows, lons), 0)
        first = jnp.where(spot < size, spot, -2).astype(F32) + 1.0
        second = jnp.where((spot >= size) & (spot < 2 * size), spot - size, -2).astype(F32) + 1.0
        moved = exact_dot(jnp.where(rank == first, 1.0, 0.0), mat)
        raw = jnp.where(rank == second, 1.0, 0.0)
        rate = table_row(tables, LAT_RATE, edge)
        toward = (table_row(tables, HEADING, edge) > 0.5) == wanted
        own = moved * (1.0 - rate) + raw
        inner = moved * jnp.where(toward, rate, 0.0)
        high, low = split(jnp.concatenate([own, inner] if is_low else [inner, own], axis=1))
        span = 2 * lons
        extra = padded(size, 16)
        out[:rows, :span] = high
        out[:rows, span:] = high
        out[rows:, :span] = jnp.where(spot_below(size, extra, span), low[:extra].astype(F32), 0.0).astype(BF16)
        out[rows:, span:] = jnp.zeros((extra, span), BF16)

    def spot_below(size, extra, span):
        return lax.broadcasted_iota(jnp.int32, (extra, span), 0) < size

    def adder(out, size, is_low):
        edge, inner = (2, 3) if is_low else (lats + 1, lats)
        mat = low_mat if is_low else high_mat
        columns = padded(2 * size, 16)

        def wide(which, at):
            tile = spread(which, at)
            return jnp.concatenate([tile, tile], axis=1)[:, :columns]

        mask = (wide(HEADING, edge) > 0.5) == is_low
        rank = jnp.where(mask, dot((across <= down).astype(BF16), mask.astype(BF16)), 0.0)
        spot = lax.broadcasted_iota(jnp.int32, (lons, columns), 1)
        first = jnp.where(spot < size, spot, -2).astype(F32) + 1.0
        second = jnp.where((spot >= size) & (spot < 2 * size), spot - size, -2).astype(F32) + 1.0
        partial = jnp.where(rank == first, 1.0, 0.0)
        raw = jnp.where(rank == second, 1.0, 0.0)
        grown = exact_dot(mat * table_row(tables, LAT_RATE, edge), raw)
        rate = wide(LAT_RATE, edge)
        here = (1.0 - rate) * grown + rate * partial
        next_in = jnp.where((wide(HEADING, inner) > 0.5) == is_low, wide(LAT_RATE, inner), 0.0) * grown
        high, low = split(jnp.concatenate([here, next_in] if is_low else [next_in, here], axis=0))
        out[:2 * lons] = high
        out[2 * lons:] = low

    def sides(cross_low):
        packer(pack_cross, kept, cross_low)
        packer(pack_chip, lons, not cross_low)
        adder(add_cross, kept, cross_low)
        adder(add_chip, lons, not cross_low)

    pl.when(blocks[0] == 0)(lambda: sides(True))
    pl.when(blocks[0] != 0)(lambda: sides(False))


def sweep_columns(value, tables, first, mats, held, emit, group):
    lons = tables.shape[-1]

    def rate(k):
        return table_row(tables, LAT_RATE, first + 2 + k)

    def sign(k):
        return table_row(tables, HEADING, first + 2 + k)

    for k in range(-1, group + 1):
        start = blend(value(k), rate(k), sign(k), value(k - 1), value(k + 1))
        both = dot(jnp.concatenate(split(start), axis=1), mats(k + 1))
        held[:, (k + 1) * lons:(k + 2) * lons] = both[:, :lons] + both[:, lons:]
        if k >= 1:
            at = (k - 1) * lons
            below, center, above = (held[:, at + s * lons:at + (s + 1) * lons] for s in range(3))
            emit(k - 1, blend(center, rate(k - 1), sign(k - 1), below, above))


def edge_choice(step, first_step, last_step, halo_low, halo_high, rows):
    def take(k, group, lons, low, main, high):
        if k < 0:
            span = slice((k + 2) * lons, (k + 3) * lons)
            inside = low[rows, span]
            return inside if halo_low is None else jnp.where(step == first_step, halo_low[rows, span], inside)
        if k < group:
            return main[rows, k * lons:(k + 1) * lons]
        span = slice((k - group) * lons, (k - group + 1) * lons)
        inside = high[rows, span]
        return inside if halo_high is None else jnp.where(step == last_step, halo_high[rows, span], inside)

    return take


def pick_mats(main, first_extra, second_extra, group):
    def mats(at):
        if at < group:
            return main[at]
        return first_extra[0] if at == group else second_extra[0]

    return mats


def pack_kernel(group, place, steps_all, with_halo, blocks, tables, mats, mats_a, mats_b, pack_cross, pack_chip, *refs):
    cross, chip = refs[0:3], refs[3:6]
    at = 10 if with_halo else 6
    halos = (refs[6:8], refs[8:10]) if with_halo else ((None, None), (None, None))
    out_cross, out_chip, held, moved = refs[at:at + 4]
    lons = tables.shape[-1]
    side = 2 * lons
    step = place(pl.program_id(0))
    chosen = [edge_choice(step, 0, steps_all - 1, *halo, slice(None)) for halo in halos]

    def value(k):
        return jnp.concatenate(
            [choose(k, group, lons, *parts) for choose, parts in zip(chosen, (cross, chip))], axis=0
        )

    def emit(k, values):
        moved[:, k * lons:(k + 1) * lons] = values

    sweep_columns(value, tables, step * group, pick_mats(mats, mats_a, mats_b, group), held, emit, group)
    for part, (packer, out) in enumerate(((pack_cross, out_cross), (pack_chip, out_chip))):
        sums = dot(packer[...], jnp.concatenate(split(moved[part * side:(part + 1) * side]), axis=0))
        count = out.shape[0]
        rows = padded(count, 16)
        extra = padded(count // 2, 16)
        out[:extra] = sums[:extra] + sums[rows:]
        out[extra:] = sums[extra:count]


def local_kernel(group, steps_all, tables, mats, mats_a, mats_b, row_mats, rates, signs, low, main, high,
                 halo_low, halo_high, out, held, moved, stage):
    lons = tables.shape[-1]
    step = pl.program_id(0)
    lats = row_mats.shape[0] - 2
    part = held.shape[0]

    def one(block, carry):
        rows = pl.ds(pl.multiple_of(block * part, part), part)
        choose = edge_choice(step, 0, steps_all - 1, halo_low, halo_high, rows)

        def emit(k, values):
            moved[rows, k * lons:(k + 1) * lons] = values

        sweep_columns(
            lambda k: choose(k, group, lons, low, main, high), tables, step * group,
            pick_mats(mats, mats_a, mats_b, group), held, emit, group,
        )
        return carry

    lax.fori_loop(0, main.shape[0] // part, one, 0)

    def wide(ref, at):
        return jnp.concatenate([ref[at]] * group, axis=1)

    def lat_of(ref, lat):
        return ref[lat * lons:(lat + 1) * lons, :]

    zero = jnp.zeros((lons, group * lons), F32)
    for lat in range(-1, lats + 1):
        near = [lat_of(moved, at) if 0 <= at < lats else zero for at in (lat - 1, lat, lat + 1)]
        start = blend(near[1], wide(rates, lat + 1), wide(signs, lat + 1), near[0], near[2])
        both = dot(row_mats[lat + 1], jnp.concatenate(split(start), axis=0))
        stage[(lat + 1) * lons:(lat + 2) * lons, :] = both[:lons] + both[lons:]
        if lat >= 1:
            done = lat - 1
            below, center, above = (lat_of(stage, done + s) for s in range(3))
            out[done * lons:(done + 1) * lons, :] = blend(
                center, wide(rates, done + 1), wide(signs, done + 1), below, above
            )


def add_kernel(blocks, adder, received, before, after):
    side = after.shape[0]
    columns = adder.shape[1]
    values = received[...]
    if values.shape[0] < columns:
        rest = jnp.zeros((columns - values.shape[0], values.shape[1]), F32)
        values = jnp.concatenate([values, rest], axis=0)
    high, low = split(values)
    both = dot(adder[...], high)
    after[...] = before[...] + (both[:side] + (both[side:] + dot(adder[:side], low)))


def params():
    return pltpu.CompilerParams(vmem_limit_bytes=VMEM_BYTES)


def whole_spec(shape):
    return pl.BlockSpec(shape, lambda *_: (0,) * len(shape))


def mats_specs(group, place, side):
    return [
        pl.BlockSpec((group, side, side), lambda g, *_: (place(g), 0, 0)),
        pl.BlockSpec((1, side, side), lambda g, *_: (place(g) * group + group, 0, 0)),
        pl.BlockSpec((1, side, side), lambda g, *_: (place(g) * group + group + 1, 0, 0)),
    ]


def window_specs(rows, row_block, group, place, lons, col_blocks):
    half = group // 2
    return [
        pl.BlockSpec((rows, 2 * lons), lambda g, *_: (row_block(*_), jnp.maximum(place(g) * half - 1, 0))),
        pl.BlockSpec((rows, group * lons), lambda g, *_: (row_block(*_), place(g))),
        pl.BlockSpec((rows, 2 * lons), lambda g, *_: (row_block(*_), jnp.minimum((place(g) + 1) * half, col_blocks - 1))),
    ]


def largest_part(total, most):
    return max(part for part in range(1, most + 1) if total % part == 0)


def cost(flops, moved):
    return pl.CostEstimate(flops=flops, bytes_accessed=moved, transcendentals=0)


def cost(flops, moved):
    return pl.CostEstimate(flops=flops, bytes_accessed=moved, transcendentals=0)


def prepare(firsts, sources, counts):
    lats, lons = sources[0].shape
    shapes = [jax.ShapeDtypeStruct((5, count, lons), F32) for count in counts]
    return pl.pallas_call(
        prepare_kernel,
        in_specs=[pl.BlockSpec(memory_space=pltpu.SMEM)] + [whole_spec(t.shape) for t in sources],
        out_specs=[whole_spec(shape.shape) for shape in shapes] + [pl.BlockSpec(memory_space=pltpu.SMEM)],
        out_shape=shapes + [jax.ShapeDtypeStruct((1,), jnp.int32)],
        scratch_shapes=[pltpu.VMEM((5, lats + 24, lons), F32)],
        compiler_params=params(),
        name="prepare",
    )(firsts, *sources)


def column_tables(tables, lons):
    total = tables.shape[1]
    return pl.pallas_call(
        column_tables_kernel,
        grid=(total // 8,),
        in_specs=[pl.BlockSpec((tables.shape[0], 8, lons), lambda g: (0, g, 0))],
        out_specs=pl.BlockSpec((8, 2 * lons, 2 * lons), lambda g: (g, 0, 0)),
        out_shape=jax.ShapeDtypeStruct((total, 2 * lons, 2 * lons), BF16),
        compiler_params=params(),
        cost_estimate=cost(0, total * 16 * lons * lons),
        name="column_tables",
    )(tables)


def row_tables(blocks, tables, lats, lons, kept):
    side = 2 * lons
    shapes = [
        jax.ShapeDtypeStruct((lats + 2, side, side), BF16),
        jax.ShapeDtypeStruct((lats + 2, lons, lons), F32),
        jax.ShapeDtypeStruct((lats + 2, lons, lons), F32),
    ]
    for size in (kept, lons):
        shapes.append(jax.ShapeDtypeStruct((padded(2 * size, 16) + padded(size, 16), 2 * side), BF16))
    for size in (kept, lons):
        shapes.append(jax.ShapeDtypeStruct((2 * side, padded(2 * size, 16)), BF16))
    return pl.pallas_call(
        functools.partial(row_tables_kernel, kept),
        in_specs=[pl.BlockSpec(memory_space=pltpu.SMEM), whole_spec(tables.shape)],
        out_specs=[whole_spec(shape.shape) for shape in shapes],
        out_shape=shapes,
        compiler_params=params(),
        name="row_tables",
    )(blocks, tables)


def pack_call(blocks, covariance, tables, mats, mats_first, packers, halos, group, chunk, kept):
    rows, cols = covariance.shape
    lons = tables.shape[-1]
    side = 2 * lons
    steps_all = cols // (group * lons)
    first, stride, steps = chunk
    with_halo = halos is not None

    def place(g):
        return first + stride * g

    def mats_place(g):
        return place(g) - mats_first

    specs = [whole_spec(tables.shape)] + mats_specs(group, mats_place, side)
    specs += [whole_spec(packer.shape) for packer in packers]
    for which in (0, 1):
        specs += window_specs(side, lambda b, w=which: b[w], group, place, lons, cols // side)
    args = [blocks, tables, mats, mats, mats, *packers] + [covariance] * 6
    if with_halo:
        for which in (0, 1):
            specs += [pl.BlockSpec((side, side), lambda g, b, w=which: (b[w], 0))] * 2
            args += list(halos)
    width = steps * group * lons
    sent = [jax.ShapeDtypeStruct((2 * size, width), F32) for size in (kept, lons)]
    return pl.pallas_call(
        functools.partial(pack_kernel, group, place, steps_all, with_halo),
        grid_spec=pltpu.PrefetchScalarGridSpec(
            num_scalar_prefetch=1,
            grid=(steps,),
            in_specs=specs,
            out_specs=[pl.BlockSpec((2 * size, group * lons), lambda g, *_: (0, g)) for size in (kept, lons)],
            scratch_shapes=[
                pltpu.VMEM((2 * side, (group + 2) * lons), F32),
                pltpu.VMEM((2 * side, group * lons), F32),
            ],
        ),
        out_shape=sent,
        compiler_params=params(),
        cost_estimate=cost(0, width * side * 16),
        name="pack_edges",
    )(*args)


def local_call(covariance, tables, mats, row_mats, rates, signs, halos, group):
    rows, cols = covariance.shape
    lons = tables.shape[-1]
    side = 2 * lons
    steps_all = cols // (group * lons)
    specs = [whole_spec(tables.shape)] + mats_specs(group, lambda g: g, side)
    specs += [whole_spec(row_mats.shape), whole_spec(rates.shape), whole_spec(signs.shape)]
    specs += window_specs(rows, lambda: 0, group, lambda g: g, lons, cols // side)
    specs += [whole_spec((rows, side))] * 2
    return pl.pallas_call(
        functools.partial(local_kernel, group, steps_all),
        grid=(steps_all,),
        in_specs=specs,
        out_specs=pl.BlockSpec((rows, group * lons), lambda g: (0, g)),
        out_shape=jax.ShapeDtypeStruct((rows, cols), F32),
        scratch_shapes=[
            pltpu.VMEM((side, (group + 2) * lons), F32),
            pltpu.VMEM((rows, group * lons), F32),
            pltpu.VMEM((rows + side, group * lons), F32),
        ],
        compiler_params=params(),
        cost_estimate=cost(0, rows * cols * 16),
        name="local_forecast",
    )(tables, mats, mats, mats, row_mats, rates, signs, covariance, covariance, covariance, *halos)


def add_call(blocks, which, forecast, adder, received, chunk, group):
    side = adder.shape[0] // 2
    width = group * side // 2
    first, stride, steps = chunk
    spot = pl.BlockSpec((side, width), lambda g, b: (b[which], first + stride * g))
    return pl.pallas_call(
        add_kernel,
        grid_spec=pltpu.PrefetchScalarGridSpec(
            num_scalar_prefetch=1,
            grid=(steps,),
            in_specs=[
                whole_spec(adder.shape),
                pl.BlockSpec((received.shape[0], width), lambda g, b: (0, g)),
                spot,
            ],
            out_specs=spot,
        ),
        out_shape=jax.ShapeDtypeStruct(forecast.shape, F32),
        input_output_aliases={3: 0},
        compiler_params=params(),
        cost_estimate=cost(0, 2 * side * steps * width * 4),
        name="add_edges",
    )(blocks, adder, received, forecast)


def neighbours(axis):
    count = lax.axis_size(axis)
    up = [(i, i + 1) for i in range(count - 1)]
    return up, [(target, source) for source, target in up]


def chunks_of(steps_all):
    if steps_all < 4:
        return [(0, 1, steps_all)]
    inner = steps_all - 2
    start = max(1, inner // 3)
    return [(1, 1, start), (1 + start, 1, inner - start), (0, steps_all - 1, 2)]


def swaps(axis, start):
    count = lax.axis_size(axis)
    pairs = [(i, i + 1) for i in range(start, count - 1, 2)]
    return pairs + [(b, a) for a, b in pairs]


def forecast_with(kept, covariance, blocks, row_part, col_part, first_part, mat_part, tall_halos):
    rows, cols = covariance.shape
    lons = row_part.shape[-1]
    group = largest_part(cols // lons, 8)
    chunks = chunks_of(cols // (group * lons))
    cross, chip = swaps("row", 1), swaps("row", 0)
    col_up, col_down = neighbours("col")
    halos = (lax.ppermute(tall_halos[0], "col", col_up), lax.ppermute(tall_halos[1], "col", col_down))
    row_mats, rates, signs, pack_cross, pack_chip, add_cross, add_chip = row_tables(
        blocks, row_part, rows // lons, lons, kept
    )
    packers = (pack_cross, pack_chip)
    early, late = (chunks[0], 1) if len(chunks) > 1 else (None, 0)
    arrived = []

    def send(chunk, mats, mats_first, packers, halos):
        to_cross, to_chip = pack_call(
            blocks, covariance, col_part, mats, mats_first, packers, halos, group, chunk, kept
        )
        arrived.append((lax.ppermute(to_cross, "row", cross), lax.ppermute(to_chip, "row", chip)))

    if early:
        send(early, column_tables(first_part, lons), early[0], packers, None)
    mats = column_tables(mat_part, lons)
    for chunk in chunks[late:-1]:
        send(chunk, mats, 0, packers, None)
    forecast = local_call(covariance, col_part, mats, row_mats, rates, signs, halos, group)
    forecast, packers = lax.optimization_barrier((forecast, packers))
    send(chunks[-1], mats, 0, packers, halos)
    for which, adder in ((1, add_chip), (0, add_cross)):
        for chunk, received in zip(chunks, arrived):
            forecast = add_call(blocks, which, forecast, adder, received[which], chunk, group)
    return forecast


def per_device(covariance, lon_courant, lat_courant, zonal_upwind_sign, lat_sign, cycle_counts):
    rows, cols = covariance.shape
    lons = lon_courant.shape[1]
    row_lats, col_lats = rows // lons, cols // lons
    group = largest_part(col_lats, 8)
    chunk = chunks_of(col_lats // group)[0]
    row = lax.axis_index("row")
    col_first = lax.axis_index("col") * col_lats
    firsts = jnp.stack([row * row_lats, col_first, col_first + chunk[0] * group]).astype(jnp.int32)
    last = rows // (2 * lons) - 1
    blocks = jnp.where(row % 2 == 0, jnp.array([0, last]), jnp.array([last, 0])).astype(jnp.int32)
    counts = (row_lats + 4, col_lats + 4, padded(chunk[2] * group + 2, 8), padded(col_lats + 2, 8))
    sources = (lon_courant, lat_courant, zonal_upwind_sign, lat_sign, cycle_counts[:, None])
    *parts, most = prepare(firsts, sources, counts)
    sizes = [lons * part // 32 for part in (19, 22, 32)]
    branch = sum((most[0] > size).astype(jnp.int32) for size in sizes[:-1])
    tall_halos = (covariance[:, cols - 2 * lons:], covariance[:, :2 * lons])
    return lax.switch(
        branch, [functools.partial(forecast_with, size) for size in sizes],
        covariance, blocks, *parts, tall_halos,
    )


def solution(mesh):
    placed = (P("row", "col"), P(), P(), P(), P(), P())
    return jax.shard_map(
        per_device, mesh=mesh, in_specs=placed, out_specs=P("row", "col"), check_vma=False
    )
```

profile of v0, /device:TPU:1, one launch (start us, length us, event | category | flops | bytes accessed | tf_op | source)
XLA Modules:
  0.0 199.2 jit_solution(13230070101526483773)
XLA Ops:
  0.0 0.6 pad_add_fusion.firsts
  0.6 1.4 copy.36.refs_4_
  2.0 1.6 prepare.1
  5.0 194.3 %conditional.1 = (f32[1024,8192]{1,0:T(8,128)}) conditional(s32[]{:T(128)} %bitcast.4, (pred[]{:T(512)}, f32[5,12,128]{2,1,0:T(8,128)S(1)}, f32[5,72,128]{2,1,0:T(8,128)S(1)}, f32[1024,8192]{1,0:T(8,128)}, f32[1024,8192]{1,0:T(8,128)}, /*index=5*/f32[5,68,128]{2,1,0:T(8,128)S(1)}, f32[1024,8192]{1,0:T(8,128)}, ...), branch_computations={%region_0.1_spmd, %region_1.2_spmd, %region_2.3_spmd} | conditional | flops 12 | bytes 339739232 | solution.py:566
  5.0 0.0 copy-start.17
  5.0 8.5 %column_tables.6.mats.mats_a.mats_b = bf16[72,256,256]{2,1,0:T(8,128)(2,1)} custom-call(f32[5,72,128]{2,1,0:T(8,128)S(1)} %get-tuple-element.61.tables), custom_call_target="tpu_custom_call" | custom-call | bytes 18874368 | tf_op jit(solution)/shard_map/cond/branch_0_fun/column_tables/pallas_call | solution.py:366
  13.5 0.0 copy-done.17
  13.5 0.5 broadcast_select_fusion.blocks
  14.0 4.5 %row_tables.3 = (bf16[10,256,256]{2,1,0:T(8,128)(2,1)}, f32[10,128,128]{2,1,0:T(8,128)}, f32[10,128,128]{2,1,0:T(8,128)}, bf16[240,512]{1,0:T(8,128)(2,1)}, bf16...) custom-call(s32[2]{0:T(128)} %broadcast_select_fusion.blocks, ...), custom_call_target="tpu_custom_call" | custom-call | tf_op jit(solution)/shard_map/cond/branch_0_fun/row_tables/pallas_call | solution.py:389
  18.5 13.1 %pack_edges.10 = (f32[152,4096]{1,0:T(8,128)}, f32[256,4096]{1,0:T(8,128)}) custom-call(s32[2]{0:T(128)} %broadcast_select_fusion.blocks, f32[5,68,128]{2,1,0:T(8,128)S(1)} %get-tuple-element.60.tables, bf16[72,256,256]{2,1,0:T(8,128)(2,1)} %column_tables.6.mats.mats_a.mats_b, bf16[72,256,256]{2,1,0:T(8,128)(2,1)} %column_tables.6.mats.mats_a.mats_b, ...), custom_call_target="tpu_custom_call" | custom-call | bytes 16777216 | tf_op jit(solution)/shard_map/cond/branch_0_fun/pack_edges/pallas_call | solution.py:424
  31.6 0.1 collective-permute-start.6
  31.8 3.3 %column_tables.7.mats.mats_a.mats_b = bf16[24,256,256]{2,1,0:T(8,128)(2,1)} custom-call(f32[5,24,128]{2,1,0:T(8,128)S(1)} %get-tuple-element.74.tables), custom_call_target="tpu_custom_call" | custom-call | bytes 6291456 | tf_op jit(solution)/shard_map/cond/branch_0_fun/column_tables/pallas_call | solution.py:366
  35.1 8.4 %pack_edges.11 = (f32[152,2048]{1,0:T(8,128)}, f32[256,2048]{1,0:T(8,128)}) custom-call(s32[2]{0:T(128)} %broadcast_select_fusion.blocks, f32[5,68,128]{2,1,0:T(8,128)S(1)} %get-tuple-element.60.tables, bf16[24,256,256]{2,1,0:T(8,128)(2,1)} %column_tables.7.mats.mats_a.mats_b, bf16[24,256,256]{2,1,0:T(8,128)(2,1)} %column_tables.7.mats.mats_a.mats_b, ...), custom_call_target="tpu_custom_call" | custom-call | bytes 8388608 | tf_op jit(solution)/shard_map/cond/branch_0_fun/pack_edges/pallas_call | solution.py:424
  43.5 0.5 collective-permute-start.7
  44.0 1.3 slice.8
  45.3 4.3 %collective-permute-start = (f32[1024,256]{1,0:T(8,128)S(1)}, f32[1024,256]{1,0:T(8,128)S(1)}, u32[]{:S(2)}, u32[]{:S(2)}) collective-permute-start(f32[1024,256]{1,0:T(8,128)S(1)} %slice.8), channel_id=1, source_target_pairs={{0,1},{2,3},{4,5},{6,7},{8,9},{10,11},{12,13},{14,15},{16,17},{18,... | collective-permute-start | bytes 3145736 | tf_op jit(solution)/shard_map/cond/branch_0_fun/ppermute | solution.py:521
  49.5 1.3 slice.11
  50.8 1.3 collective-permute-start.1
  52.1 3.9 %collective-permute-start.3 = (f32[152,4096]{1,0:T(8,128)}, f32[152,4096]{1,0:T(8,128)}, u32[]{:S(2)}, u32[]{:S(2)}) collective-permute-start(f32[152,4096]{1,0:T(8,128)} %get-tuple-element.73), channel_id=1, source_target_pairs={{2,4},{6,8},{10,12},{14,16},{18,20},{22,24},{26,28},{4,2},{8,6},{1... | collective-permute-start | bytes 7471112 | tf_op jit(solution)/shard_map/cond/branch_0_fun/ppermute | solution.py:533
  56.1 15.4 %collective-permute-done.halo_low.refs_6_.refs_8_ = f32[1024,256]{1,0:T(8,128)S(1)} collective-permute-done((f32[1024,256]{1,0:T(8,128)S(1)}, f32[1024,256]{1,0:T(8,128)S(1)}, u32[]{:S(2)}, u32[]{:S(2)}) %collective-permute-start) | collective-permute-done | bytes 1048608 | tf_op jit(solution)/shard_map/cond/branch_0_fun/ppermute | solution.py:521
  71.5 0.0 copy-start
  71.5 5.2 %collective-permute-done.1.halo_high.refs_7_.refs_9_ = f32[1024,256]{1,0:T(8,128)S(1)} collective-permute-done((f32[1024,256]{1,0:T(8,128)S(1)}, f32[1024,256]{1,0:T(8,128)S(1)}, u32[]{:S(2)}, u32[]{:S(2)}) %collective-permute-start.1) | collective-permute-done | bytes 1048608 | tf_op jit(solution)/shard_map/cond/branch_0_fun/ppermute | solution.py:521
  76.7 0.0 copy-start.2
  76.7 0.0 copy-done
  76.7 1.0 copy-done.2
  77.7 48.6 %local_forecast.3.before = f32[1024,8192]{1,0:T(8,128)} custom-call(f32[5,68,128]{2,1,0:T(8,128)S(1)} %get-tuple-element.60.tables, bf16[72,256,256]{2,1,0:T(8,128)(2,1)} %column_tables.6.mats.mats_a.mats_b, bf16[72,256,256]{2,1,0:T(8,128)(2,1)} %column_tables.6.mats.mats_a.mats_b, bf16[72,256,256]{2,1,0:T(8,128)(2,1)} %column_tables.6.mats.mats_a.mats_b, ...), custom_call_target="tpu_custom_call" | custom-call | bytes 134217728 | tf_op jit(solution)/shard_map/cond/branch_0_fun/local_forecast/pallas_call | solution.py:452
  126.2 0.0 copy-start.20
  126.2 8.9 %pack_edges.9 = (f32[152,2048]{1,0:T(8,128)}, f32[256,2048]{1,0:T(8,128)}) custom-call(s32[2]{0:T(128)} %broadcast_select_fusion.blocks, f32[5,68,128]{2,1,0:T(8,128)S(1)} %get-tuple-element.60.tables, bf16[72,256,256]{2,1,0:T(8,128)(2,1)} %column_tables.6.mats.mats_a.mats_b, bf16[72,256,256]{2,1,0:T(8,128)(2,1)} %column_tables.6.mats.mats_a.mats_b, ...), custom_call_target="tpu_custom_call" | custom-call | bytes 8388608 | tf_op jit(solution)/shard_map/cond/branch_0_fun/pack_edges/pallas_call | solution.py:424
  135.2 1.7 collective-permute-start.5
  136.9 0.0 copy-done.20
  136.9 3.0 %collective-permute-start.4 = (f32[152,2048]{1,0:T(8,128)S(1)}, f32[152,2048]{1,0:T(8,128)S(1)}, u32[]{:S(2)}, u32[]{:S(2)}) collective-permute-start(f32[152,2048]{1,0:T(8,128)S(1)} %copy-done.20), channel_id=1, source_target_pairs={{2,4},{6,8},{10,12},{14,16},{18,20},{22,24},{26,28},{4,2},{8,6},{1... | collective-permute-start | bytes 3735560 | tf_op jit(solution)/shard_map/cond/branch_0_fun/ppermute | solution.py:533
  139.9 0.0 collective-permute-done.7.received
  139.9 0.0 copy-start.6
  139.9 2.5 %collective-permute-start.2 = (f32[152,2048]{1,0:T(8,128)}, f32[152,2048]{1,0:T(8,128)S(1)}, u32[]{:S(2)}, u32[]{:S(2)}) collective-permute-start(f32[152,2048]{1,0:T(8,128)} %get-tuple-element.72), channel_id=1, source_target_pairs={{2,4},{6,8},{10,12},{14,16},{18,20},{22,24},{26,28},{4,2},{8,6},{1... | collective-permute-start | bytes 3735560 | tf_op jit(solution)/shard_map/cond/branch_0_fun/ppermute | solution.py:533
  142.4 0.0 copy-done.6
  142.5 4.5 %add_edges.18.before = f32[1024,8192]{1,0:T(8,128)} custom-call(s32[2]{0:T(128)} %broadcast_select_fusion.blocks, bf16[512,256]{1,0:T(8,128)(2,1)} %get-tuple-element.76.adder, f32[256,2048]{1,0:T(8,128)} %copy-done.6, f32[1024,8192]{1,0:T(8,128)} %local_forecast.3.before), custom_call_target="tpu_custom_call", output_to_operand_aliasing={{}: (3, {})} | custom-call | bytes 4194304 | tf_op jit(solution)/shard_map/cond/branch_0_fun/add_edges/pallas_call | solution.py:474
  147.0 0.0 collective-permute-done.6.received
  147.0 7.4 %add_edges.19.before = f32[1024,8192]{1,0:T(8,128)} custom-call(s32[2]{0:T(128)} %broadcast_select_fusion.blocks, bf16[512,256]{1,0:T(8,128)(2,1)} %get-tuple-element.76.adder, f32[256,4096]{1,0:T(8,128)} %collective-permute-done.6.received, f32[1024,8192]{1,0:T(8,128)} %add_edges.18.before), custom_call_target="tpu_custom_call", output_to_operand_aliasing={{}: (3, {})} | custom-call | bytes 8388608 | tf_op jit(solution)/shard_map/cond/branch_0_fun/add_edges/pallas_call | solution.py:474
  154.4 0.0 collective-permute-done.5.received
  154.4 0.0 copy-start.11
  154.4 1.4 copy-done.11
  155.7 4.5 %add_edges.20.before = f32[1024,8192]{1,0:T(8,128)} custom-call(s32[2]{0:T(128)} %broadcast_select_fusion.blocks, bf16[512,256]{1,0:T(8,128)(2,1)} %get-tuple-element.76.adder, f32[256,2048]{1,0:T(8,128)} %copy-done.11, f32[1024,8192]{1,0:T(8,128)} %add_edges.19.before), custom_call_target="tpu_custom_call", output_to_operand_aliasing={{}: (3, {})} | custom-call | bytes 4194304 | tf_op jit(solution)/shard_map/cond/branch_0_fun/add_edges/pallas_call | solution.py:474
  160.2 20.2 %collective-permute-done.4.received = f32[152,2048]{1,0:T(8,128)S(1)} collective-permute-done((f32[152,2048]{1,0:T(8,128)S(1)}, f32[152,2048]{1,0:T(8,128)S(1)}, u32[]{:S(2)}, u32[]{:S(2)}) %collective-permute-start.4) | collective-permute-done | bytes 1245216 | tf_op jit(solution)/shard_map/cond/branch_0_fun/ppermute | solution.py:533
  180.4 0.0 copy-start.16
  180.4 1.0 copy-done.16
  181.4 4.3 %add_edges.21.before = f32[1024,8192]{1,0:T(8,128)} custom-call(s32[2]{0:T(128)} %broadcast_select_fusion.blocks, bf16[512,160]{1,0:T(8,128)(2,1)} %get-tuple-element.59.adder, f32[152,2048]{1,0:T(8,128)} %copy-done.16, f32[1024,8192]{1,0:T(8,128)} %add_edges.20.before), custom_call_target="tpu_custom_call", output_to_operand_aliasing={{}: (3, {})} | custom-call | bytes 4194304 | tf_op jit(solution)/shard_map/cond/branch_0_fun/add_edges/pallas_call | solution.py:474
  185.7 0.0 collective-permute-done.3.received
  185.7 7.0 %add_edges.22.before = f32[1024,8192]{1,0:T(8,128)} custom-call(s32[2]{0:T(128)} %broadcast_select_fusion.blocks, bf16[512,160]{1,0:T(8,128)(2,1)} %get-tuple-element.59.adder, f32[152,4096]{1,0:T(8,128)} %collective-permute-done.3.received, f32[1024,8192]{1,0:T(8,128)} %add_edges.21.before), custom_call_target="tpu_custom_call", output_to_operand_aliasing={{}: (3, {})} | custom-call | bytes 8388608 | tf_op jit(solution)/shard_map/cond/branch_0_fun/add_edges/pallas_call | solution.py:474
  192.7 1.1 collective-permute-done.2.received
  193.8 0.0 copy-start.15
  193.8 1.1 copy-done.15
  194.9 4.3 %add_edges.23 = f32[1024,8192]{1,0:T(8,128)} custom-call(s32[2]{0:T(128)} %broadcast_select_fusion.blocks, bf16[512,160]{1,0:T(8,128)(2,1)} %get-tuple-element.59.adder, f32[152,2048]{1,0:T(8,128)} %copy-done.15, f32[1024,8192]{1,0:T(8,128)} %add_edges.22.before), custom_call_target="tpu_custom_call", output_to_operand_aliasing={{}: (3, {})} | custom-call | bytes 4194304 | tf_op jit(solution)/shard_map/cond/branch_0_fun/add_edges/pallas_call | solution.py:474
  (1 shorter events, 0.0 us)
Async XLA Ops:
  5.0 8.5 %copy-start.17 = (s32[2]{0:T(128)S(1)}, s32[2]{0:T(128)}, u32[]{:S(2)}) copy-start(s32[2]{0:T(128)} %constant.42.clone.1) | copy-start | bytes 28 | tf_op jit(solution)/shard_map/cond
  31.6 115.3 %collective-permute-start.6 = (f32[256,4096]{1,0:T(8,128)}, f32[256,4096]{1,0:T(8,128)}, u32[]{:S(2)}, u32[]{:S(2)}) collective-permute-start(f32[256,4096]{1,0:T(8,128)} %get-tuple-element.78), channel_id=1, source_target_pairs={{0,2},{4,6},{8,10},{12,14},{16,18},{20,22},{24,26},{28,30},{2,0},{... | collective-permute-start | bytes 12582920 | tf_op jit(solution)/shard_map/cond/branch_0_fun/ppermute | solution.py:533
  43.5 96.4 %collective-permute-start.7 = (f32[256,2048]{1,0:T(8,128)}, f32[256,2048]{1,0:T(8,128)S(1)}, u32[]{:S(2)}, u32[]{:S(2)}) collective-permute-start(f32[256,2048]{1,0:T(8,128)} %get-tuple-element.79), channel_id=1, source_target_pairs={{0,2},{4,6},{8,10},{12,14},{16,18},{20,22},{24,26},{28,30},{2,0},{... | collective-permute-start | bytes 6291464 | tf_op jit(solution)/shard_map/cond/branch_0_fun/ppermute | solution.py:533
  45.3 26.2 %collective-permute-start = (f32[1024,256]{1,0:T(8,128)S(1)}, f32[1024,256]{1,0:T(8,128)S(1)}, u32[]{:S(2)}, u32[]{:S(2)}) collective-permute-start(f32[1024,256]{1,0:T(8,128)S(1)} %slice.8), channel_id=1, source_target_pairs={{0,1},{2,3},{4,5},{6,7},{8,9},{10,11},{12,13},{14,15},{16,17},{18,... | collective-permute-start | bytes 3145736 | tf_op jit(solution)/shard_map/cond/branch_0_fun/ppermute | solution.py:521
  50.8 25.8 %collective-permute-start.1 = (f32[1024,256]{1,0:T(8,128)S(1)}, f32[1024,256]{1,0:T(8,128)S(1)}, u32[]{:S(2)}, u32[]{:S(2)}) collective-permute-start(f32[1024,256]{1,0:T(8,128)S(1)} %slice.11), channel_id=1, source_target_pairs={{1,0},{3,2},{5,4},{7,6},{9,8},{11,10},{13,12},{15,14},{17,16},{19,... | collective-permute-start | bytes 3145736 | tf_op jit(solution)/shard_map/cond/branch_0_fun/ppermute | solution.py:521
  52.1 133.6 %collective-permute-start.3 = (f32[152,4096]{1,0:T(8,128)}, f32[152,4096]{1,0:T(8,128)}, u32[]{:S(2)}, u32[]{:S(2)}) collective-permute-start(f32[152,4096]{1,0:T(8,128)} %get-tuple-element.73), channel_id=1, source_target_pairs={{2,4},{6,8},{10,12},{14,16},{18,20},{22,24},{26,28},{4,2},{8,6},{1... | collective-permute-start | bytes 7471112 | tf_op jit(solution)/shard_map/cond/branch_0_fun/ppermute | solution.py:533
  71.5 5.2 %copy-start = (f32[1024,256]{1,0:T(8,128)}, f32[1024,256]{1,0:T(8,128)S(1)}, u32[]{:S(2)}) copy-start(f32[1024,256]{1,0:T(8,128)S(1)} %collective-permute-done.halo_low.refs_6_.refs_8_) | copy-start | bytes 3145732 | tf_op jit(solution)/shard_map/cond
  76.7 1.0 copy-start.2
  126.2 10.6 %copy-start.20 = (f32[152,2048]{1,0:T(8,128)S(1)}, f32[152,2048]{1,0:T(8,128)}, u32[]{:S(2)}) copy-start(f32[152,2048]{1,0:T(8,128)} %get-tuple-element.75) | copy-start | bytes 3735556 | tf_op jit(solution)/shard_map/cond
  135.2 19.2 %collective-permute-start.5 = (f32[256,2048]{1,0:T(8,128)}, f32[256,2048]{1,0:T(8,128)S(1)}, u32[]{:S(2)}, u32[]{:S(2)}) collective-permute-start(f32[256,2048]{1,0:T(8,128)} %get-tuple-element.77), channel_id=1, source_target_pairs={{0,2},{4,6},{8,10},{12,14},{16,18},{20,22},{24,26},{28,30},{2,0},{... | collective-permute-start | bytes 6291464 | tf_op jit(solution)/shard_map/cond/branch_0_fun/ppermute | solution.py:533
  136.9 43.5 %collective-permute-start.4 = (f32[152,2048]{1,0:T(8,128)S(1)}, f32[152,2048]{1,0:T(8,128)S(1)}, u32[]{:S(2)}, u32[]{:S(2)}) collective-permute-start(f32[152,2048]{1,0:T(8,128)S(1)} %copy-done.20), channel_id=1, source_target_pairs={{2,4},{6,8},{10,12},{14,16},{18,20},{22,24},{26,28},{4,2},{8,6},{1... | collective-permute-start | bytes 3735560 | tf_op jit(solution)/shard_map/cond/branch_0_fun/ppermute | solution.py:533
  139.9 2.5 %copy-start.6 = (f32[256,2048]{1,0:T(8,128)}, f32[256,2048]{1,0:T(8,128)S(1)}, u32[]{:S(2)}) copy-start(f32[256,2048]{1,0:T(8,128)S(1)} %collective-permute-done.7.received) | copy-start | bytes 6291460 | tf_op jit(solution)/shard_map/cond
  139.9 53.9 %collective-permute-start.2 = (f32[152,2048]{1,0:T(8,128)}, f32[152,2048]{1,0:T(8,128)S(1)}, u32[]{:S(2)}, u32[]{:S(2)}) collective-permute-start(f32[152,2048]{1,0:T(8,128)} %get-tuple-element.72), channel_id=1, source_target_pairs={{2,4},{6,8},{10,12},{14,16},{18,20},{22,24},{26,28},{4,2},{8,6},{1... | collective-permute-start | bytes 3735560 | tf_op jit(solution)/shard_map/cond/branch_0_fun/ppermute | solution.py:533
  154.4 1.4 copy-start.11
  180.4 1.0 copy-start.16
  193.8 1.1 copy-start.15
where the time goes:
time: 200 us; the launch traced here: 199 us
  Pallas kernels  129 us (64%)
  waiting for transfers between devices  41.9 us (21%)
  starting transfers between devices  17.4 us (9%)
  local copies, waits for them, and re-layouts  8.47 us (4%)
    pallas_call x1, Pallas kernels, local_call(): pl.pallas_call(functools.partial(local_kernel, group, steps_all), grid=(s...  48.6 us
    pallas_call x6, Pallas kernels, add_call(): pl.pallas_call(add_kernel, grid_spec=pltpu.PrefetchScalarGridSpec(num_sca...  32 us
    pallas_call x3, Pallas kernels, pack_call(): pl.pallas_call(functools.partial(pack_kernel, group, place, steps_all, wi...  30.4 us
    ppermute x3, waiting for transfers between devices, send(): lax.ppermute(to_cross, 'row', cross)  21.3 us
    ppermute x1, waiting for transfers between devices, forecast_with(): lax.ppermute(tall_halos[0], 'col', col_up)  15.4 us
    pallas_call x2, Pallas kernels, column_tables(): pl.pallas_call(column_tables_kernel, grid=(total // 8,), in_specs=[pl.Blo...  11.8 us
    ppermute x3, starting transfers between devices, send(): lax.ppermute(to_cross, 'row', cross)  9.48 us
    ppermute x1, waiting for transfers between devices, forecast_with(): lax.ppermute(tall_halos[1], 'col', col_down)  5.16 us
  transfers between devices with their start and end apart: 8, of which 4 were waited for; matrix products, arithmetic and copies ran while one was open for 1% of the time, Pallas kernels for 49%

commit v1 on v0

--- a/solution.py
+++ b/solution.py
@@ -96,7 +96,7 @@
     most[0] = jnp.max(needed).astype(jnp.int32)
 
 
-def row_tables_kernel(kept, blocks, tables, mats, rates, signs, pack_cross, pack_chip, add_cross, add_chip):
+def row_tables_kernel(kept, blocks, tables, mats, rates, signs, pack_cross, add_cross):
     lons = tables.shape[-1]
     lats = mats.shape[0] - 2
     square = (lons, lons)
@@ -177,9 +177,7 @@
 
     def sides(cross_low):
         packer(pack_cross, kept, cross_low)
-        packer(pack_chip, lons, not cross_low)
         adder(add_cross, kept, cross_low)
-        adder(add_chip, lons, not cross_low)
 
     pl.when(blocks[0] == 0)(lambda: sides(True))
     pl.when(blocks[0] != 0)(lambda: sides(False))
@@ -228,65 +226,77 @@
     return mats
 
 
-def pack_kernel(group, place, steps_all, with_halo, blocks, tables, mats, mats_a, mats_b, pack_cross, pack_chip, *refs):
-    cross, chip = refs[0:3], refs[3:6]
-    at = 10 if with_halo else 6
-    halos = (refs[6:8], refs[8:10]) if with_halo else ((None, None), (None, None))
-    out_cross, out_chip, held, moved = refs[at:at + 4]
-    lons = tables.shape[-1]
-    side = 2 * lons
+def pack_kernel(group, place, steps_all, blocks, tables, mats, mats_a, mats_b, packer, low, main, high, *refs):
+    halos = refs[:2] if len(refs) == 5 else (None, None)
+    out, held, moved = refs[-3:]
+    lons = tables.shape[-1]
     step = place(pl.program_id(0))
-    chosen = [edge_choice(step, 0, steps_all - 1, *halo, slice(None)) for halo in halos]
-
-    def value(k):
-        return jnp.concatenate(
-            [choose(k, group, lons, *parts) for choose, parts in zip(chosen, (cross, chip))], axis=0
-        )
+    choose = edge_choice(step, 0, steps_all - 1, *halos, slice(None))
 
     def emit(k, values):
         moved[:, k * lons:(k + 1) * lons] = values
 
-    sweep_columns(value, tables, step * group, pick_mats(mats, mats_a, mats_b, group), held, emit, group)
-    for part, (packer, out) in enumerate(((pack_cross, out_cross), (pack_chip, out_chip))):
-        sums = dot(packer[...], jnp.concatenate(split(moved[part * side:(part + 1) * side]), axis=0))
-        count = out.shape[0]
-        rows = padded(count, 16)
-        extra = padded(count // 2, 16)
-        out[:extra] = sums[:extra] + sums[rows:]
-        out[extra:] = sums[extra:count]
-
-
-def local_kernel(group, steps_all, tables, mats, mats_a, mats_b, row_mats, rates, signs, low, main, high,
-                 halo_low, halo_high, out, held, moved, stage):
-    lons = tables.shape[-1]
+    sweep_columns(
+        lambda k: choose(k, group, lons, low, main, high), tables, step * group,
+        pick_mats(mats, mats_a, mats_b, group), held, emit, group,
+    )
+    sums = dot(packer[...], jnp.concatenate(split(moved[...]), axis=0))
+    count = out.shape[0]
+    rows = padded(count, 16)
+    extra = padded(count // 2, 16)
+    out[:extra] = sums[:extra] + sums[rows:]
+    out[extra:] = sums[extra:count]
+
+
+def local_kernel(group, steps_all, blocks, tables, mats, mats_a, mats_b, row_mats, rates, signs, low, main, high,
+                 halo_low, halo_high, chip_low, chip_main, chip_high, chip_halos, out, held, moved, stage):
+    lons = tables.shape[-1]
+    side = 2 * lons
     step = pl.program_id(0)
     lats = row_mats.shape[0] - 2
     part = held.shape[0]
+    weights = pick_mats(mats, mats_a, mats_b, group)
+    chip_above = blocks[1] > 0
+    top = (lats + 2) * lons
+
+    @pl.when(step == 0)
+    def _():
+        moved[pl.ds(pl.multiple_of(jnp.where(chip_above, 0, top), lons), side), :] = jnp.zeros(
+            (side, group * lons), F32
+        )
+
+    def sweep(value, held_here, first_row, count):
+        def emit(k, values):
+            moved[pl.ds(first_row, count), k * lons:(k + 1) * lons] = values
+
+        sweep_columns(value, tables, step * group, weights, held_here, emit, group)
 
     def one(block, carry):
-        rows = pl.ds(pl.multiple_of(block * part, part), part)
-        choose = edge_choice(step, 0, steps_all - 1, halo_low, halo_high, rows)
-
-        def emit(k, values):
-            moved[rows, k * lons:(k + 1) * lons] = values
-
-        sweep_columns(
-            lambda k: choose(k, group, lons, low, main, high), tables, step * group,
-            pick_mats(mats, mats_a, mats_b, group), held, emit, group,
+        first_row = pl.multiple_of(block * part, part)
+        choose = edge_choice(step, 0, steps_all - 1, halo_low, halo_high, pl.ds(first_row, part))
+        sweep(
+            lambda k: choose(k, group, lons, low, main, high), held,
+            pl.multiple_of(first_row + side, side), part,
         )
         return carry
 
     lax.fori_loop(0, main.shape[0] // part, one, 0)
+    choose_chip = edge_choice(
+        step, 0, steps_all - 1, chip_halos.at[:, :side], chip_halos.at[:, side:], slice(None)
+    )
+    sweep(
+        lambda k: choose_chip(k, group, lons, chip_low, chip_main, chip_high), held.at[:side],
+        pl.multiple_of(jnp.where(chip_above, top, 0), lons), side,
+    )
 
     def wide(ref, at):
         return jnp.concatenate([ref[at]] * group, axis=1)
 
-    def lat_of(ref, lat):
-        return ref[lat * lons:(lat + 1) * lons, :]
-
-    zero = jnp.zeros((lons, group * lons), F32)
+    def lat_of(ref, at):
+        return ref[at * lons:(at + 1) * lons, :]
+
     for lat in range(-1, lats + 1):
-        near = [lat_of(moved, at) if 0 <= at < lats else zero for at in (lat - 1, lat, lat + 1)]
+        near = [lat_of(moved, at) for at in (lat + 1, lat + 2, lat + 3)]
         start = blend(near[1], wide(rates, lat + 1), wide(signs, lat + 1), near[0], near[2])
         both = dot(row_mats[lat + 1], jnp.concatenate(split(start), axis=0))
         stage[(lat + 1) * lons:(lat + 2) * lons, :] = both[:lons] + both[lons:]
@@ -337,14 +347,6 @@
 
 def largest_part(total, most):
     return max(part for part in range(1, most + 1) if total % part == 0)
-
-
-def cost(flops, moved):
-    return pl.CostEstimate(flops=flops, bytes_accessed=moved, transcendentals=0)
-
-
-def cost(flops, moved):
-    return pl.CostEstimate(flops=flops, bytes_accessed=moved, transcendentals=0)
 
 
 def prepare(firsts, sources, counts):
@@ -370,7 +372,6 @@
         out_specs=pl.BlockSpec((8, 2 * lons, 2 * lons), lambda g: (g, 0, 0)),
         out_shape=jax.ShapeDtypeStruct((total, 2 * lons, 2 * lons), BF16),
         compiler_params=params(),
-        cost_estimate=cost(0, total * 16 * lons * lons),
         name="column_tables",
     )(tables)
 
@@ -382,10 +383,8 @@
         jax.ShapeDtypeStruct((lats + 2, lons, lons), F32),
         jax.ShapeDtypeStruct((lats + 2, lons, lons), F32),
     ]
-    for size in (kept, lons):
-        shapes.append(jax.ShapeDtypeStruct((padded(2 * size, 16) + padded(size, 16), 2 * side), BF16))
-    for size in (kept, lons):
-        shapes.append(jax.ShapeDtypeStruct((2 * side, padded(2 * size, 16)), BF16))
+    shapes.append(jax.ShapeDtypeStruct((padded(2 * kept, 16) + padded(kept, 16), 2 * side), BF16))
+    shapes.append(jax.ShapeDtypeStruct((2 * side, padded(2 * kept, 16)), BF16))
     return pl.pallas_call(
         functools.partial(row_tables_kernel, kept),
         in_specs=[pl.BlockSpec(memory_space=pltpu.SMEM), whole_spec(tables.shape)],
@@ -396,13 +395,12 @@
     )(blocks, tables)
 
 
-def pack_call(blocks, covariance, tables, mats, mats_first, packers, halos, group, chunk, kept):
+def pack_call(blocks, covariance, tables, mats, mats_first, packer, halos, group, chunk, kept):
     rows, cols = covariance.shape
     lons = tables.shape[-1]
     side = 2 * lons
     steps_all = cols // (group * lons)
     first, stride, steps = chunk
-    with_halo = halos is not None
 
     def place(g):
         return first + stride * g
@@ -410,67 +408,69 @@
     def mats_place(g):
         return place(g) - mats_first
 
-    specs = [whole_spec(tables.shape)] + mats_specs(group, mats_place, side)
-    specs += [whole_spec(packer.shape) for packer in packers]
-    for which in (0, 1):
-        specs += window_specs(side, lambda b, w=which: b[w], group, place, lons, cols // side)
-    args = [blocks, tables, mats, mats, mats, *packers] + [covariance] * 6
-    if with_halo:
-        for which in (0, 1):
-            specs += [pl.BlockSpec((side, side), lambda g, b, w=which: (b[w], 0))] * 2
-            args += list(halos)
-    width = steps * group * lons
-    sent = [jax.ShapeDtypeStruct((2 * size, width), F32) for size in (kept, lons)]
+    specs = [whole_spec(tables.shape)] + mats_specs(group, mats_place, side) + [whole_spec(packer.shape)]
+    specs += window_specs(side, lambda b: b[0], group, place, lons, cols // side)
+    args = [blocks, tables, mats, mats, mats, packer] + [covariance] * 3
+    if halos is not None:
+        specs += [pl.BlockSpec((side, side), lambda g, b: (b[0], 0))] * 2
+        args += list(halos)
     return pl.pallas_call(
-        functools.partial(pack_kernel, group, place, steps_all, with_halo),
+        functools.partial(pack_kernel, group, place, steps_all),
         grid_spec=pltpu.PrefetchScalarGridSpec(
             num_scalar_prefetch=1,
             grid=(steps,),
             in_specs=specs,
-            out_specs=[pl.BlockSpec((2 * size, group * lons), lambda g, *_: (0, g)) for size in (kept, lons)],
+            out_specs=pl.BlockSpec((2 * kept, group * lons), lambda g, *_: (0, g)),
             scratch_shapes=[
-                pltpu.VMEM((2 * side, (group + 2) * lons), F32),
-                pltpu.VMEM((2 * side, group * lons), F32),
+                pltpu.VMEM((side, (group + 2) * lons), F32),
+                pltpu.VMEM((side, group * lons), F32),
             ],
         ),
-        out_shape=sent,
+        out_shape=jax.ShapeDtypeStruct((2 * kept, steps * group * lons), F32),
         compiler_params=params(),
-        cost_estimate=cost(0, width * side * 16),
         name="pack_edges",
     )(*args)
 
 
-def local_call(covariance, tables, mats, row_mats, rates, signs, halos, group):
+def local_call(blocks, covariance, tables, mats, row_mats, rates, signs, halos, chip_rows, chip_halos, group):
     rows, cols = covariance.shape
     lons = tables.shape[-1]
     side = 2 * lons
     steps_all = cols // (group * lons)
+    part = largest_part(rows // side, 2) * side
     specs = [whole_spec(tables.shape)] + mats_specs(group, lambda g: g, side)
     specs += [whole_spec(row_mats.shape), whole_spec(rates.shape), whole_spec(signs.shape)]
-    specs += window_specs(rows, lambda: 0, group, lambda g: g, lons, cols // side)
+    specs += window_specs(rows, lambda *_: 0, group, lambda g: g, lons, cols // side)
     specs += [whole_spec((rows, side))] * 2
+    specs += window_specs(side, lambda *_: 0, group, lambda g: g, lons, cols // side)
+    specs += [whole_spec(chip_halos.shape)]
     return pl.pallas_call(
         functools.partial(local_kernel, group, steps_all),
-        grid=(steps_all,),
-        in_specs=specs,
-        out_specs=pl.BlockSpec((rows, group * lons), lambda g: (0, g)),
+        grid_spec=pltpu.PrefetchScalarGridSpec(
+            num_scalar_prefetch=1,
+            grid=(steps_all,),
+            in_specs=specs,
+            out_specs=pl.BlockSpec((rows, group * lons), lambda g, *_: (0, g)),
+            scratch_shapes=[
+                pltpu.VMEM((part, (group + 2) * lons), F32),
+                pltpu.VMEM((rows + 2 * side, group * lons), F32),
+                pltpu.VMEM((rows + side, group * lons), F32),
+            ],
+        ),
         out_shape=jax.ShapeDtypeStruct((rows, cols), F32),
-        scratch_shapes=[
-            pltpu.VMEM((side, (group + 2) * lons), F32),
-            pltpu.VMEM((rows, group * lons), F32),
-            pltpu.VMEM((rows + side, group * lons), F32),
-        ],
         compiler_params=params(),
-        cost_estimate=cost(0, rows * cols * 16),
         name="local_forecast",
-    )(tables, mats, mats, mats, row_mats, rates, signs, covariance, covariance, covariance, *halos)
-
-
-def add_call(blocks, which, forecast, adder, received, chunk, group):
+    )(
+        blocks, tables, mats, mats, mats, row_mats, rates, signs, covariance, covariance, covariance, *halos,
+        chip_rows, chip_rows, chip_rows, chip_halos,
+    )
+
+
+def add_call(blocks, forecast, adder, received, chunk, group):
     side = adder.shape[0] // 2
     width = group * side // 2
     first, stride, steps = chunk
-    spot = pl.BlockSpec((side, width), lambda g, b: (b[which], first + stride * g))
+    spot = pl.BlockSpec((side, width), lambda g, b: (b[0], first + stride * g))
     return pl.pallas_call(
         add_kernel,
         grid_spec=pltpu.PrefetchScalarGridSpec(
@@ -486,7 +486,6 @@
         out_shape=jax.ShapeDtypeStruct(forecast.shape, F32),
         input_output_aliases={3: 0},
         compiler_params=params(),
-        cost_estimate=cost(0, 2 * side * steps * width * 4),
         name="add_edges",
     )(blocks, adder, received, forecast)
 
@@ -511,38 +510,47 @@
     return pairs + [(b, a) for a, b in pairs]
 
 
-def forecast_with(kept, covariance, blocks, row_part, col_part, first_part, mat_part, tall_halos):
+def forecast_with(kept, covariance, blocks, spots, row_part, col_part, first_part, mat_part):
     rows, cols = covariance.shape
     lons = row_part.shape[-1]
+    side = 2 * lons
     group = largest_part(cols // lons, 8)
     chunks = chunks_of(cols // (group * lons))
     cross, chip = swaps("row", 1), swaps("row", 0)
     col_up, col_down = neighbours("col")
-    halos = (lax.ppermute(tall_halos[0], "col", col_up), lax.ppermute(tall_halos[1], "col", col_down))
-    row_mats, rates, signs, pack_cross, pack_chip, add_cross, add_chip = row_tables(
-        blocks, row_part, rows // lons, lons, kept
-    )
-    packers = (pack_cross, pack_chip)
-    early, late = (chunks[0], 1) if len(chunks) > 1 else (None, 0)
+    row_mats, rates, signs, packer, adder = row_tables(blocks, row_part, rows // lons, lons, kept)
     arrived = []
 
-    def send(chunk, mats, mats_first, packers, halos):
-        to_cross, to_chip = pack_call(
-            blocks, covariance, col_part, mats, mats_first, packers, halos, group, chunk, kept
-        )
-        arrived.append((lax.ppermute(to_cross, "row", cross), lax.ppermute(to_chip, "row", chip)))
-
+    def pack(chunk, mats, mats_first, halos):
+        return pack_call(blocks, covariance, col_part, mats, mats_first, packer, halos, group, chunk, kept)
+
+    def send(packed):
+        arrived.append(lax.ppermute(packed, "row", cross))
+
+    early = len(chunks) > 1
     if early:
-        send(early, column_tables(first_part, lons), early[0], packers, None)
+        packed = pack(chunks[0], column_tables(first_part, lons), chunks[0][0], None)
+        packed, mat_part, spots = lax.optimization_barrier((packed, mat_part, spots))
+        send(packed)
+    tall_low = lax.dynamic_slice(covariance, (spots[0], spots[0] + cols - side), (rows, side))
+    tall_high = lax.dynamic_slice(covariance, (spots[0], spots[0]), (rows, side))
+    halos = (lax.ppermute(tall_low, "col", col_up), lax.ppermute(tall_high, "col", col_down))
+    chip_rows = lax.ppermute(lax.dynamic_slice(covariance, (spots[1], spots[0]), (side, cols)), "row", chip)
     mats = column_tables(mat_part, lons)
-    for chunk in chunks[late:-1]:
-        send(chunk, mats, 0, packers, None)
-    forecast = local_call(covariance, col_part, mats, row_mats, rates, signs, halos, group)
-    forecast, packers = lax.optimization_barrier((forecast, packers))
-    send(chunks[-1], mats, 0, packers, halos)
-    for which, adder in ((1, add_chip), (0, add_cross)):
-        for chunk, received in zip(chunks, arrived):
-            forecast = add_call(blocks, which, forecast, adder, received[which], chunk, group)
+    for chunk in chunks[early:-1]:
+        packed, arrived[0], halos = lax.optimization_barrier((pack(chunk, mats, 0, None), arrived[0], halos))
+        send(packed)
+    near = [lax.dynamic_slice(halo, (spots[1], spots[0]), (side, side)) for halo in halos]
+    chip_halos = lax.ppermute(jnp.concatenate(near, axis=1), "row", chip)
+    packed = pack(chunks[-1], mats, 0, halos)
+    packed, row_mats = lax.optimization_barrier((packed, row_mats))
+    send(packed)
+    forecast = local_call(
+        blocks, covariance, col_part, mats, row_mats, rates, signs, halos, chip_rows, chip_halos, group
+    )
+    order = [0, 2, 1] if len(chunks) == 3 else range(len(chunks))
+    for at in order:
+        forecast = add_call(blocks, forecast, adder, arrived[at], chunks[at], group)
     return forecast
 
 
@@ -562,10 +570,10 @@
     *parts, most = prepare(firsts, sources, counts)
     sizes = [lons * part // 32 for part in (19, 22, 32)]
     branch = sum((most[0] > size).astype(jnp.int32) for size in sizes[:-1])
-    tall_halos = (covariance[:, cols - 2 * lons:], covariance[:, :2 * lons])
+    spots = jnp.stack([jnp.zeros_like(row), blocks[1] * 2 * lons]).astype(jnp.int32)
     return lax.switch(
         branch, [functools.partial(forecast_with, size) for size in sizes],
-        covariance, blocks, *parts, tall_halos,
+        covariance, blocks, spots, *parts,
     )
 
 

time: 200 us -> 167 us (0.83)
  waiting for transfers between devices: 41.9 us -> 15.2 us
  Pallas kernels: 129 us -> 107 us
  local copies, waits for them, and re-layouts: 8.47 us -> 17.6 us
  loops' own time: 0.13 us -> 5.24 us
    ppermute x8 -> x7, waiting for transfers between devices: 41.9 us -> 15.2 us  [the longest x3 9.71 us: send(): arrived.append(lax.ppermute(packed, 'row', cross))]
    pallas_call x6 -> x3, Pallas kernels: 32 us -> 15.2 us  [add_call(): pl.pallas_call(add_kernel, grid_spec=pltpu.PrefetchScalarGridSpec(num_sca...]
    dynamic_slice x0 -> x3, local copies, waits for them, and re-layouts: none -> 11.7 us  [the longest x1 8.28 us: forecast_with(): lax.dynamic_slice(covariance, (spots[1], spots[0]), (side, cols))]
    another operation x1, loops' own time: 0.13 us -> 5.24 us  [per_device(): lax.switch(branch, [functools.partial(forecast_with, size) for size in si...]
    pallas_call x4, Pallas kernels: 79 us -> 74.8 us  [the longest x1 55.4 us: local_call(): pl.pallas_call(functools.partial(local_kernel, group, steps_all), grid_sp...]
    cond x16 -> x14, local copies, waits for them, and re-layouts: 4.49 us -> 3.32 us
    ppermute x8 -> x7, starting transfers between devices: 17.4 us -> 17 us  [the longest x3 11.5 us: send(): arrived.append(lax.ppermute(packed, 'row', cross))]
  transfers between devices with their start and end apart: 8 -> 7, of which waited for: 4 -> 4; matrix products, arithmetic and copies ran while one was open for 1% -> 2% of each run, Pallas kernels for 49% -> 52%
where the time goes in v1:
time: 167 us; the launch traced here: 166 us
  Pallas kernels  107 us (64%)
  local copies, waits for them, and re-layouts  17.6 us (11%)
  starting transfers between devices  17 us (10%)
  waiting for transfers between devices  15.2 us (9%)
  loops' own time  5.24 us (3%)
  between operations  2.01 us (1%)
    pallas_call x1, Pallas kernels, local_call(): pl.pallas_call(functools.partial(local_kernel, group, steps_all), grid_sp...  55.4 us
    pallas_call x3, Pallas kernels, pack_call(): pl.pallas_call(functools.partial(pack_kernel, group, place, steps_all), g...  19.4 us
    pallas_call x3, Pallas kernels, add_call(): pl.pallas_call(add_kernel, grid_spec=pltpu.PrefetchScalarGridSpec(num_sca...  15.2 us
    pallas_call x2, Pallas kernels, column_tables(): pl.pallas_call(column_tables_kernel, grid=(total // 8,), in_specs=[pl.Blo...  11.8 us
    ppermute x3, starting transfers between devices, send(): arrived.append(lax.ppermute(packed, 'row', cross))  11.5 us
    ppermute x3, waiting for transfers between devices, send(): arrived.append(lax.ppermute(packed, 'row', cross))  9.71 us
    dynamic_slice x1, local copies, waits for them, and re-layouts, forecast_with(): lax.dynamic_slice(covariance, (spots[1], spots[0]), (side, cols))  8.28 us
    another operation x1, loops' own time, per_device(): lax.switch(branch, [functools.partial(forecast_with, size) for size in si...  5.24 us
  transfers between devices with their start and end apart: 7, of which 4 were waited for; matrix products, arithmetic and copies ran while one was open for 2% of the time, Pallas kernels for 52%

profile of v1, /device:TPU:1, one launch (start us, length us, event | category | flops | bytes accessed | tf_op | source)
XLA Modules:
  0.0 165.8 jit_solution(2219619000762073633)
XLA Ops:
  0.0 0.6 pad_add_fusion.firsts
  0.6 0.7 broadcast_select_fusion
  1.3 0.6 slice.24
  2.5 0.1 pad_add_fusion.1
  2.6 1.4 copy.24.refs_4_
  4.0 1.6 prepare.1
  7.0 158.8 %conditional.1 = (f32[1024,8192]{1,0:T(8,128)}) conditional(s32[]{:T(128)} %bitcast.10, (s32[2]{0:T(128)S(1)}, f32[5,12,128]{2,1,0:T(8,128)S(1)}, f32[5,24,128]{2,1,0:T(8,128)S(1)}, f32[5,68,128]{2,1,0:T(8,128)S(1)}, f32[1024,8192]{1,0:T(8,128)}, /*index=5*/f32[5,72,128]{2,1,0:T(8,128)S(1)}, s32[2]{0:T(128)S(1)}) %tuple.23, ...), branch_computations={%region_0.1_spmd, %region_1.2_spmd, %region_2.3_spmd} | conditional | flops 131082 | bytes 129401456 | solution.py:574
  7.0 3.4 %column_tables.6.mats.mats_a.mats_b = bf16[24,256,256]{2,1,0:T(8,128)(2,1)} custom-call(f32[5,24,128]{2,1,0:T(8,128)S(1)} %get-tuple-element.55.tables), custom_call_target="tpu_custom_call" | custom-call | tf_op jit(solution)/shard_map/cond/branch_0_fun/column_tables/pallas_call | solution.py:368
  10.4 4.0 %row_tables.3 = (bf16[10,256,256]{2,1,0:T(8,128)(2,1)}, f32[10,128,128]{2,1,0:T(8,128)}, f32[10,128,128]{2,1,0:T(8,128)}, bf16[240,512]{1,0:T(8,128)(2,1)}, bf16[512,160]{1,0:T(8,128)(2,1)}) custom-call(s32[2]{0:T(128)S(1)} %get-tuple-element.50.blocks, f32[5,12,128]{2,1,0:T(8,128)S(1)} %get-tuple-element.52.tables), custom_call_target="tpu_custom_call" | custom-call | tf_op jit(solution)/shard_map/cond/branch_0_fun/row_tables/pallas_call | solution.py:388
  14.3 5.3 %pack_edges.9 = f32[152,2048]{1,0:T(8,128)} custom-call(s32[2]{0:T(128)S(1)} %get-tuple-element.50.blocks, f32[5,68,128]{2,1,0:T(8,128)S(1)} %get-tuple-element.54.tables, bf16[24,256,256]{2,1,0:T(8,128)(2,1)} %column_tables.6.mats.mats_a.mats_b, bf16[24,256,256]{2,1,0:T(8,128)(2,1)} %column_tables.6.mats.mats_a.mats_b, ...), custom_call_target="tpu_custom_call" | custom-call | tf_op jit(solution)/shard_map/cond/branch_0_fun/pack_edges/pallas_call | solution.py:417
  19.6 0.6 fusion
  22.2 0.0 copy-start.15
  22.2 8.3 %constant_dynamic-slice_fusion.2 = f32[256,8192]{1,0:T(8,128)} fusion(f32[1024,8192]{1,0:T(8,128)} %get-tuple-element.128.low.main.high, s32[]{:T(128)S(6)} %select_n.33), kind=kLoop, calls=%fused_computation.3 | loop fusion | bytes 16777220 | tf_op jit(solution)/shard_map/cond/branch_0_fun/dynamic_slice | solution.py:538
  30.5 0.0 collective-permute-start.5
  30.5 0.0 copy-done.15
  30.5 4.3 %collective-permute-start = (f32[152,2048]{1,0:T(8,128)S(1)}, f32[152,2048]{1,0:T(8,128)S(1)}, u32[]{:S(2)}, u32[]{:S(2)}) collective-permute-start(f32[152,2048]{1,0:T(8,128)S(1)} %copy-done.15), channel_id=1, source_target_pairs={{2,4},{6,8},{10,12},{14,16},{18,20},{22,24},{26,28},{4,2},{8,6},{1... | collective-permute-start | bytes 3735560 | tf_op jit(solution)/shard_map/cond/branch_0_fun/ppermute | solution.py:528
  38.0 2.3 %constant_dynamic-slice_fusion.3 = (f32[1024,256]{1,0:T(8,128)S(1)}, f32[1024,256]{1,0:T(8,128)S(1)}) fusion(f32[1024,8192]{1,0:T(8,128)} %get-tuple-element.128.low.main.high, s32[]{:T(128)S(6)} %select_n.32, s32[]{:T(128)S(6)} %select_n.31), kind=kLoop, calls=%fused_computation.4 | loop fusion | bytes 4194312 | tf_op jit(solution)/shard_map/cond/branch_0_fun/dynamic_slice | solution.py:536
  40.3 1.3 collective-permute-start.2
  41.6 4.1 %collective-permute-start.1 = (f32[1024,256]{1,0:T(8,128)S(1)}, f32[1024,256]{1,0:T(8,128)S(1)}, u32[]{:S(2)}, u32[]{:S(2)}) collective-permute-start(f32[1024,256]{1,0:T(8,128)S(1)} %get-tuple-element.132), channel_id=1, source_target_pairs={{0,1},{2,3},{4,5},{6,7},{8,9},{10,11},{12,13},{14,15},{16,17},{18,... | collective-permute-start | bytes 3145736 | tf_op jit(solution)/shard_map/cond/branch_0_fun/ppermute | solution.py:537
  45.7 8.4 %column_tables.7.mats.mats_a.mats_b = bf16[72,256,256]{2,1,0:T(8,128)(2,1)} custom-call(f32[5,72,128]{2,1,0:T(8,128)S(1)} %get-tuple-element.60.tables), custom_call_target="tpu_custom_call" | custom-call | tf_op jit(solution)/shard_map/cond/branch_0_fun/column_tables/pallas_call | solution.py:368
  54.2 8.5 %pack_edges.10 = f32[152,4096]{1,0:T(8,128)} custom-call(s32[2]{0:T(128)S(1)} %get-tuple-element.50.blocks, f32[5,68,128]{2,1,0:T(8,128)S(1)} %get-tuple-element.54.tables, bf16[72,256,256]{2,1,0:T(8,128)(2,1)} %column_tables.7.mats.mats_a.mats_b, bf16[72,256,256]{2,1,0:T(8,128)(2,1)} %column_tables.7.mats.mats_a.mats_b, ...), custom_call_target="tpu_custom_call" | custom-call | tf_op jit(solution)/shard_map/cond/branch_0_fun/pack_edges/pallas_call | solution.py:417
  62.7 1.8 %collective-permute-done.2.refs_1_.halo_high = f32[1024,256]{1,0:T(8,128)S(1)} collective-permute-done((f32[1024,256]{1,0:T(8,128)S(1)}, f32[1024,256]{1,0:T(8,128)S(1)}, u32[]{:S(2)}, u32[]{:S(2)}) %collective-permute-start.2) | collective-permute-done | bytes 1048608 | tf_op jit(solution)/shard_map/cond/branch_0_fun/ppermute | solution.py:537
  64.4 0.0 copy-start
  64.5 1.8 %collective-permute-done.1.refs_0_.halo_low = f32[1024,256]{1,0:T(8,128)S(1)} collective-permute-done((f32[1024,256]{1,0:T(8,128)S(1)}, f32[1024,256]{1,0:T(8,128)S(1)}, u32[]{:S(2)}, u32[]{:S(2)}) %collective-permute-start.1) | collective-permute-done | bytes 1048608 | tf_op jit(solution)/shard_map/cond/branch_0_fun/ppermute | solution.py:537
  66.3 0.0 copy-start.3
  66.3 0.0 collective-permute-done.received
  66.3 0.0 copy-start.14
  66.3 5.1 %collective-permute-start.3 = (f32[152,4096]{1,0:T(8,128)}, f32[152,4096]{1,0:T(8,128)S(1)}, u32[]{:S(2)}, u32[]{:S(2)}) collective-permute-start(f32[152,4096]{1,0:T(8,128)} %pack_edges.10), channel_id=1, source_target_pairs={{2,4},{6,8},{10,12},{14,16},{18,20},{22,24},{26,28},{4,2},{8,6},{1... | collective-permute-start | bytes 7471112 | tf_op jit(solution)/shard_map/cond/branch_0_fun/ppermute | solution.py:528
  71.4 0.0 copy-done
  71.4 0.0 copy-done.3
  71.4 5.6 %pack_edges.11 = f32[152,2048]{1,0:T(8,128)} custom-call(s32[2]{0:T(128)S(1)} %get-tuple-element.50.blocks, f32[5,68,128]{2,1,0:T(8,128)S(1)} %get-tuple-element.54.tables, bf16[72,256,256]{2,1,0:T(8,128)(2,1)} %column_tables.7.mats.mats_a.mats_b, bf16[72,256,256]{2,1,0:T(8,128)(2,1)} %column_tables.7.mats.mats_a.mats_b, ...), custom_call_target="tpu_custom_call" | custom-call | tf_op jit(solution)/shard_map/cond/branch_0_fun/pack_edges/pallas_call | solution.py:417
  76.9 0.0 copy-done.14
  76.9 2.1 %collective-permute-start.4 = (f32[152,2048]{1,0:T(8,128)}, f32[152,2048]{1,0:T(8,128)S(1)}, u32[]{:S(2)}, u32[]{:S(2)}) collective-permute-start(f32[152,2048]{1,0:T(8,128)} %pack_edges.11), channel_id=1, source_target_pairs={{2,4},{6,8},{10,12},{14,16},{18,20},{22,24},{26,28},{4,2},{8,6},{1... | collective-permute-start | bytes 3735560 | tf_op jit(solution)/shard_map/cond/branch_0_fun/ppermute | solution.py:528
  79.1 1.1 constant_dynamic-slice_fusion
  80.1 0.1 pad_maximum_fusion
  80.2 0.1 collective-permute-start.6
  80.3 1.9 %collective-permute-done.6.chip_halos = f32[256,512]{1,0:T(8,128)S(1)} collective-permute-done((f32[256,512]{1,0:T(8,128)S(1)}, f32[256,512]{1,0:T(8,128)S(1)}, u32[]{:S(2)}, u32[]{:S(2)}) %collective-permute-start.6) | collective-permute-done | bytes 524320 | tf_op jit(solution)/shard_map/cond/branch_0_fun/ppermute | solution.py:544
  82.2 0.0 copy-start.17
  82.2 0.0 collective-permute-done.5.chip_low.chip_main.chip_high
  82.2 0.8 copy-done.17
  83.0 55.4 %local_forecast.3.before = f32[1024,8192]{1,0:T(8,128)} custom-call(s32[2]{0:T(128)S(1)} %get-tuple-element.50.blocks, f32[5,68,128]{2,1,0:T(8,128)S(1)} %get-tuple-element.54.tables, bf16[72,256,256]{2,1,0:T(8,128)(2,1)} %column_tables.7.mats.mats_a.mats_b, bf16[72,256,256]{2,1,0:T(8,128)(2,1)} %column_tables.7.mats.mats_a.mats_b, ...), custom_call_target="tpu_custom_call" | custom-call | tf_op jit(solution)/shard_map/cond/branch_0_fun/local_forecast/pallas_call | solution.py:447
  138.4 4.2 %add_edges.9.before = f32[1024,8192]{1,0:T(8,128)} custom-call(s32[2]{0:T(128)S(1)} %get-tuple-element.50.blocks, bf16[512,160]{1,0:T(8,128)(2,1)} %get-tuple-element.53.adder, f32[152,2048]{1,0:T(8,128)} %copy-done.14, f32[1024,8192]{1,0:T(8,128)} %local_forecast.3.before), custom_call_target="tpu_custom_call", output_to_operand_aliasing={{}: (3, {})} | custom-call | tf_op jit(solution)/shard_map/cond/branch_0_fun/add_edges/pallas_call | solution.py:474
  142.5 9.7 %collective-permute-done.4.received = f32[152,2048]{1,0:T(8,128)S(1)} collective-permute-done((f32[152,2048]{1,0:T(8,128)}, f32[152,2048]{1,0:T(8,128)S(1)}, u32[]{:S(2)}, u32[]{:S(2)}) %collective-permute-start.4) | collective-permute-done | bytes 1245216 | tf_op jit(solution)/shard_map/cond/branch_0_fun/ppermute | solution.py:528
  152.2 0.0 copy-start.16
  152.2 1.1 copy-done.16
  153.3 4.2 %add_edges.10.before = f32[1024,8192]{1,0:T(8,128)} custom-call(s32[2]{0:T(128)S(1)} %get-tuple-element.50.blocks, bf16[512,160]{1,0:T(8,128)(2,1)} %get-tuple-element.53.adder, f32[152,2048]{1,0:T(8,128)} %copy-done.16, f32[1024,8192]{1,0:T(8,128)} %add_edges.9.before), custom_call_target="tpu_custom_call", output_to_operand_aliasing={{}: (3, {})} | custom-call | tf_op jit(solution)/shard_map/cond/branch_0_fun/add_edges/pallas_call | solution.py:474
  157.5 0.0 collective-permute-done.3.received
  157.5 0.0 copy-start.7
  157.5 1.4 copy-done.7
  158.9 6.9 %add_edges.11 = f32[1024,8192]{1,0:T(8,128)} custom-call(s32[2]{0:T(128)S(1)} %get-tuple-element.50.blocks, bf16[512,160]{1,0:T(8,128)(2,1)} %get-tuple-element.53.adder, f32[152,4096]{1,0:T(8,128)} %copy-done.7, f32[1024,8192]{1,0:T(8,128)} %add_edges.10.before), custom_call_target="tpu_custom_call", output_to_operand_aliasing={{}: (3, {})} | custom-call | tf_op jit(solution)/shard_map/cond/branch_0_fun/add_edges/pallas_call | solution.py:474
Async XLA Ops:
  22.2 8.3 %copy-start.15 = (f32[152,2048]{1,0:T(8,128)S(1)}, f32[152,2048]{1,0:T(8,128)}, u32[]{:S(2)}) copy-start(f32[152,2048]{1,0:T(8,128)} %pack_edges.9) | copy-start | bytes 3735556 | tf_op jit(solution)/shard_map/cond
  30.5 51.7 %collective-permute-start.5 = (f32[256,8192]{1,0:T(8,128)}, f32[256,8192]{1,0:T(8,128)}, u32[]{:S(2)}, u32[]{:S(2)}) collective-permute-start(f32[256,8192]{1,0:T(8,128)} %constant_dynamic-slice_fusion.2), channel_id=1, source_target_pairs={{0,2},{4,6},{8,10},{12,14},{16,18},{20,22},{24,26},{28,30},{2,0},{... | collective-permute-start | bytes 25165832 | tf_op jit(solution)/shard_map/cond/branch_0_fun/ppermute | solution.py:538
  30.5 35.8 %collective-permute-start = (f32[152,2048]{1,0:T(8,128)S(1)}, f32[152,2048]{1,0:T(8,128)S(1)}, u32[]{:S(2)}, u32[]{:S(2)}) collective-permute-start(f32[152,2048]{1,0:T(8,128)S(1)} %copy-done.15), channel_id=1, source_target_pairs={{2,4},{6,8},{10,12},{14,16},{18,20},{22,24},{26,28},{4,2},{8,6},{1... | collective-permute-start | bytes 3735560 | tf_op jit(solution)/shard_map/cond/branch_0_fun/ppermute | solution.py:528
  40.3 24.1 %collective-permute-start.2 = (f32[1024,256]{1,0:T(8,128)S(1)}, f32[1024,256]{1,0:T(8,128)S(1)}, u32[]{:S(2)}, u32[]{:S(2)}) collective-permute-start(f32[1024,256]{1,0:T(8,128)S(1)} %get-tuple-element.131), channel_id=1, source_target_pairs={{1,0},{3,2},{5,4},{7,6},{9,8},{11,10},{13,12},{15,14},{17,16},{19,... | collective-permute-start | bytes 3145736 | tf_op jit(solution)/shard_map/cond/branch_0_fun/ppermute | solution.py:537
  41.6 24.7 %collective-permute-start.1 = (f32[1024,256]{1,0:T(8,128)S(1)}, f32[1024,256]{1,0:T(8,128)S(1)}, u32[]{:S(2)}, u32[]{:S(2)}) collective-permute-start(f32[1024,256]{1,0:T(8,128)S(1)} %get-tuple-element.132), channel_id=1, source_target_pairs={{0,1},{2,3},{4,5},{6,7},{8,9},{10,11},{12,13},{14,15},{16,17},{18,... | collective-permute-start | bytes 3145736 | tf_op jit(solution)/shard_map/cond/branch_0_fun/ppermute | solution.py:537
  64.4 6.9 %copy-start = (f32[1024,256]{1,0:T(8,128)}, f32[1024,256]{1,0:T(8,128)S(1)}, u32[]{:S(2)}) copy-start(f32[1024,256]{1,0:T(8,128)S(1)} %collective-permute-done.2.refs_1_.halo_high) | copy-start | bytes 3145732 | tf_op jit(solution)/shard_map/cond
  66.3 5.1 %copy-start.3 = (f32[1024,256]{1,0:T(8,128)}, f32[1024,256]{1,0:T(8,128)S(1)}, u32[]{:S(2)}) copy-start(f32[1024,256]{1,0:T(8,128)S(1)} %collective-permute-done.1.refs_0_.halo_low) | copy-start | bytes 3145732 | tf_op jit(solution)/shard_map/cond
  66.3 10.7 %copy-start.14 = (f32[152,2048]{1,0:T(8,128)}, f32[152,2048]{1,0:T(8,128)S(1)}, u32[]{:S(2)}) copy-start(f32[152,2048]{1,0:T(8,128)S(1)} %collective-permute-done.received) | copy-start | bytes 3735556 | tf_op jit(solution)/shard_map/cond
  66.3 91.2 %collective-permute-start.3 = (f32[152,4096]{1,0:T(8,128)}, f32[152,4096]{1,0:T(8,128)S(1)}, u32[]{:S(2)}, u32[]{:S(2)}) collective-permute-start(f32[152,4096]{1,0:T(8,128)} %pack_edges.10), channel_id=1, source_target_pairs={{2,4},{6,8},{10,12},{14,16},{18,20},{22,24},{26,28},{4,2},{8,6},{1... | collective-permute-start | bytes 7471112 | tf_op jit(solution)/shard_map/cond/branch_0_fun/ppermute | solution.py:528
  76.9 75.3 %collective-permute-start.4 = (f32[152,2048]{1,0:T(8,128)}, f32[152,2048]{1,0:T(8,128)S(1)}, u32[]{:S(2)}, u32[]{:S(2)}) collective-permute-start(f32[152,2048]{1,0:T(8,128)} %pack_edges.11), channel_id=1, source_target_pairs={{2,4},{6,8},{10,12},{14,16},{18,20},{22,24},{26,28},{4,2},{8,6},{1... | collective-permute-start | bytes 3735560 | tf_op jit(solution)/shard_map/cond/branch_0_fun/ppermute | solution.py:528
  80.2 2.0 %collective-permute-start.6 = (f32[256,512]{1,0:T(8,128)S(1)}, f32[256,512]{1,0:T(8,128)S(1)}, u32[]{:S(2)}, u32[]{:S(2)}) collective-permute-start(f32[256,512]{1,0:T(8,128)S(1)} %pad_maximum_fusion), channel_id=1, source_target_pairs={{0,2},{4,6},{8,10},{12,14},{16,18},{20,22},{24,26},{28,30},{2,0},{... | collective-permute-start | bytes 1572872 | tf_op jit(solution)/shard_map/cond/branch_0_fun/ppermute | solution.py:544
  82.2 0.8 copy-start.17
  152.2 1.1 copy-start.16
  157.5 1.4 copy-start.7
